TPU v7x, 512 devices: a whole 4x4x16 slice. The times are simulated.
512 devices in a mesh: dom: 64 (over x, z), sub: 8 (over y, core).
Axes of the slice: x: 4, y: 4, z: 16, core: 2. Of those that a mesh axis runs over, the one named last changes fastest.
Arguments:
- right_side: float32 [1024, 16, 128], P(('dom', 'sub')), as said below
- diag_blocks: float32 [1024, 128, 128], P(('dom', 'sub')), as said below
- block_values: float32 [1024, 4, 128, 128], P(('dom', 'sub')), as said below
- block_cols: int32 [1024, 4], P(('dom', 'sub')), may hold values from 0 to 31, as said below
- block_count: int32 [1024], P(('dom', 'sub')), may hold values from 0 to 4, as said below
- cell_diagonal: float32 [1024, 128], P(('dom', 'sub')), as said below
Outputs:
- solution_field: float32 [1024, 16, 128], P(('dom', 'sub'))
- residual: float32 [1024, 16, 128], P(('dom', 'sub'))
Inputs may be any that keep to these rules, and one draw needn't show every extreme that they name: `block_cols`: live slots of a block row point to distinct block rows that come after it in the window (positions 0 to 15 are the block rows of the same index of dom, the rest those of the next index); block rows of the last index of dom point only into their own index; dead slots hold 0. `block_count`: the number of live slots, which varies from device to device. `block_values`: entries lie between -1 / 128 and 0. `diag_blocks`: entries lie between -1 / 128 and 0. `cell_diagonal`: every entry exceeds 1 + the live slots of its block row + the live slots of all block rows that couple to its block row, so the operator is strictly diagonally dominant. `right_side`: entries lie between -50 and 50.
All inputs are finite; a program needn't handle non-finite values.
Results may differ from a plain program's by a relative error of at most 0.00065.
Values sent between devices are 32-bit elements; how exact they have to be, the bound alone decides.
A program may use at most 64 MiB of HBM per device.

v0:
```python
import jax
import jax.numpy as jnp
from jax import lax
from jax.sharding import PartitionSpec as P

K = 4
ITERS = 3
PRECISE = lax.Precision.HIGHEST


def passed_along(x, axis, by):
    peers = lax.axis_size(axis)
    pairs = [(i, i + by) for i in range(peers) if 0 <= i + by < peers]
    return lax.ppermute(x, axis, pairs)


def local(right_side, diag_blocks, block_values, block_cols, block_count, cell_diagonal):
    rows_dev = right_side.shape[0]
    group_rows = lax.axis_size("sub") * rows_dev
    upper_part = jnp.triu(diag_blocks, 1)
    live_slots = jnp.arange(K, dtype=jnp.int32)[None, :] < block_count[:, None]
    window_ids = jnp.arange(2 * group_rows, dtype=jnp.int32)
    picker = (
        (block_cols[:, :, None] == window_ids[None, None, :]) & live_slots[:, :, None]
    ).astype(jnp.float32)

    def local_dots(first, second):
        return jnp.sum(first * second, axis=(0, 2))

    def residual_sum(residual_now, precond_now):
        return lax.psum(local_dots(residual_now, precond_now), ("dom", "sub"))

    solution_field = jnp.zeros_like(right_side)
    residual = right_side
    precond_res = residual / cell_diagonal[:, None, :]
    direction = precond_res
    precond_dot = residual_sum(residual, precond_res)
    for iteration in range(ITERS):
        own_part = jnp.einsum("rab,rzb->rza", upper_part, direction, precision=PRECISE)
        own_part = own_part + jnp.einsum("rba,rzb->rza", upper_part, direction, precision=PRECISE)
        own_part = own_part + cell_diagonal[:, None, :] * direction
        own_group = lax.all_gather(direction, "sub", axis=0, tiled=True)
        next_group = passed_along(own_group, "dom", -1)
        window = jnp.concatenate([own_group, next_group], axis=0)
        far_rows = jnp.einsum("rkw,wzb->rkzb", picker, window, precision=PRECISE)
        forward = jnp.einsum("rkab,rkzb->rza", block_values, far_rows, precision=PRECISE)
        back_terms = jnp.einsum("rkba,rzb->rkza", block_values, direction, precision=PRECISE)
        spread = jnp.einsum("rkw,rkza->wza", picker, back_terms, precision=PRECISE)
        incoming = passed_along(spread[group_rows:], "dom", 1)
        back_own = lax.psum_scatter(
            spread[:group_rows] + incoming, "sub", scatter_dimension=0, tiled=True
        )
        image_vec = own_part + forward + back_own
        curvature = lax.psum(local_dots(direction, image_vec), ("dom", "sub"))
        step_size = precond_dot / curvature
        solution_field = solution_field + step_size[None, :, None] * direction
        residual = residual - step_size[None, :, None] * image_vec
        if iteration + 1 < ITERS:
            precond_res = residual / cell_diagonal[:, None, :]
            new_dot = residual_sum(residual, precond_res)
            direction = precond_res + (new_dot / precond_dot)[None, :, None] * direction
            precond_dot = new_dot
    return (solution_field, residual)


def solution(mesh):
    return jax.shard_map(
        local,
        mesh=mesh,
        in_specs=(
            P(("dom", "sub"), None, None),
            P(("dom", "sub"), None, None),
            P(("dom", "sub"), None, None, None),
            P(("dom", "sub"), None),
            P(("dom", "sub")),
            P(("dom", "sub"), None),
        ),
        out_specs=(P(("dom", "sub"), None, None), P(("dom", "sub"), None, None)),
        check_vma=False,
    )
```

profile of v0, /device:TPU:1, one launch (start us, length us, event | category | flops | bytes accessed | tf_op | source)
XLA Modules:
  0.0 715.4 jit_solution(11586665640421009732)
XLA Ops:
  7.2 0.8 broadcast_divide_fusion
  8.0 19.6 %all_gather.9 = f32[16,16,128]{2,1,0:T(8,128)S(1)} all-gather(f32[2,16,128]{2,1,0:T(8,128)S(1)} %broadcast_divide_fusion), channel_id=1, replica_groups=mesh['dom'=64,'sub'=8] {'sub'}, dimensions={0}, use_global_device_ids=true | all-gather | bytes 147456 | tf_op jit(solution)/shard_map/all_gather | solution.py:42
  27.6 1.4 collective-permute-start
  30.3 4.0 collective-permute-start.1
  35.0 1.7 collective-permute-done.1
  36.7 0.7 copy_add_fusion.2
  37.5 0.5 convolution_bitcast_fusion.5
  38.2 37.2 %reduce-scatter.4.cloned.1.call-done = f32[2,16,128]{2,1,0:T(8,128)} async-done(((f32[16,16,128]{2,1,0:T(8,128)}), f32[2,16,128]{2,1,0:T(8,128)}) %reduce-scatter.4.cloned.1.call-update) | async-done | bytes 16400 | tf_op jit(solution)/shard_map/reduce_scatter | solution.py:50
  75.4 0.8 multiply_reduce_fusion.4
  76.2 105.7 %all-reduce = (f32[16]{0:T(128)S(1)}, f32[16]{0:T(128)S(1)}) all-reduce(f32[16]{0:T(128)S(1)} %get-tuple-element.3, f32[16]{0:T(128)S(1)} %get-tuple-element.2), channel_id=1, replica_groups=mesh['dom'=64,'sub'=8] {'dom','sub'}, use_global_device_ids=true, to_apply=%region_1.2 | all-reduce | flops 32 | bytes 256 | tf_op jit(solution)/shard_map/psum | solution.py:31
  182.2 99.4 %psum.44 = f32[16]{0:T(128)S(1)} all-reduce(f32[16]{0:T(128)S(1)} %get-tuple-element.12), channel_id=1, replica_groups=mesh['dom'=64,'sub'=8] {'dom','sub'}, use_global_device_ids=true, to_apply=%region_6.7 | all-reduce | flops 16 | bytes 128 | tf_op jit(solution)/shard_map/psum | solution.py:31
  281.7 13.2 %all_gather.10 = f32[16,16,128]{2,1,0:T(8,128)S(1)} all-gather(f32[2,16,128]{2,1,0:T(8,128)S(1)} %multiply_add_fusion.2), channel_id=1, replica_groups=mesh['dom'=64,'sub'=8] {'sub'}, dimensions={0}, use_global_device_ids=true | all-gather | bytes 147456 | tf_op jit(solution)/shard_map/all_gather | solution.py:42
  295.3 1.3 collective-permute-start.2
  297.1 4.0 collective-permute-start.3
  301.3 0.7 collective-permute-done.2
  302.4 1.0 collective-permute-done.3
  303.4 0.7 copy_add_fusion.1
  304.2 0.5 convolution_bitcast_fusion.4
  305.0 33.6 %reduce-scatter.6.cloned.1.call-done = f32[2,16,128]{2,1,0:T(8,128)} async-done(((f32[16,16,128]{2,1,0:T(8,128)}), f32[2,16,128]{2,1,0:T(8,128)}) %reduce-scatter.6.cloned.1.call-update) | async-done | bytes 16400 | tf_op jit(solution)/shard_map/reduce_scatter | solution.py:50
  338.5 0.8 multiply_reduce_fusion.2
  339.4 105.7 %psum.45 = f32[16]{0:T(128)S(1)} all-reduce(f32[16]{0:T(128)S(1)} %get-tuple-element.10), channel_id=1, replica_groups=mesh['dom'=64,'sub'=8] {'dom','sub'}, use_global_device_ids=true, to_apply=%region_9.10 | all-reduce | flops 16 | bytes 128 | tf_op jit(solution)/shard_map/psum | solution.py:54
  445.3 99.2 %psum.46 = f32[16]{0:T(128)S(1)} all-reduce(f32[16]{0:T(128)S(1)} %get-tuple-element.8), channel_id=1, replica_groups=mesh['dom'=64,'sub'=8] {'dom','sub'}, use_global_device_ids=true, to_apply=%region_11.12 | all-reduce | flops 16 | bytes 128 | tf_op jit(solution)/shard_map/psum | solution.py:31
  544.6 13.2 %all_gather.11 = f32[16,16,128]{2,1,0:T(8,128)S(1)} all-gather(f32[2,16,128]{2,1,0:T(8,128)S(1)} %multiply_add_fusion.1), channel_id=1, replica_groups=mesh['dom'=64,'sub'=8] {'sub'}, dimensions={0}, use_global_device_ids=true | all-gather | bytes 147456 | tf_op jit(solution)/shard_map/all_gather | solution.py:42
  558.2 1.3 collective-permute-start.4
  560.0 4.0 collective-permute-start.5
  564.2 0.7 collective-permute-done.4
  565.3 1.0 collective-permute-done.5
  566.3 0.7 copy_add_fusion
  567.8 33.7 %reduce-scatter.8.cloned.1.call-done = f32[2,16,128]{2,1,0:T(8,128)} async-done(((f32[16,16,128]{2,1,0:T(8,128)}), f32[2,16,128]{2,1,0:T(8,128)}) %reduce-scatter.8.cloned.1.call-update) | async-done | bytes 16400 | tf_op jit(solution)/shard_map/reduce_scatter | solution.py:50
  601.5 0.8 multiply_reduce_fusion
  602.4 105.8 %psum.47 = f32[16]{0:T(128)S(1)} all-reduce(f32[16]{0:T(128)S(1)} %get-tuple-element.6), channel_id=1, replica_groups=mesh['dom'=64,'sub'=8] {'dom','sub'}, use_global_device_ids=true, to_apply=%region_14.15 | all-reduce | flops 16 | bytes 128 | tf_op jit(solution)/shard_map/psum | solution.py:54
  708.2 0.7 multiply_subtract_fusion
  (55 shorter events, 6.7 us)
Async XLA Ops:
  7.2 21.9 %copy-start = (f32[2,4,128,128]{3,2,1,0:T(8,128)S(1)}, f32[2,4,128,128]{3,2,1,0:T(8,128)}, u32[]{:S(2)}) copy-start(f32[2,4,128,128]{3,2,1,0:T(8,128)} %param.8) | copy-start | bytes 1572868
  7.2 68.2 %reduce-scatter.4.cloned.1.call-start = ((), (), s32[]{:S(2)}) async-start(), calls=%async_computation.3 | async-start | bytes 147456 | tf_op jit(solution)/shard_map/reduce_scatter | solution.py:50
  8.0 21.0 %copy-start.5 = (s32[2]{0:T(128)S(1)}, s32[2]{0:T(128)}, u32[]{:S(2)}) copy-start(s32[2]{0:T(128)} %param.10) | copy-start | bytes 28
  8.0 21.1 %copy-start.2 = (f32[2,16,128]{2,1,0:T(8,128)S(1)}, f32[2,16,128]{2,1,0:T(8,128)}, u32[]{:S(2)}) copy-start(f32[2,16,128]{2,1,0:T(8,128)} %param.6) | copy-start | bytes 49156
  27.6 1.5 copy-start.3
  27.6 7.0 collective-permute-start
  29.1 0.7 copy-start.4
  30.2 4.1 copy-start.1
  30.3 6.4 collective-permute-start.1
  37.4 301.1 %reduce-scatter.6.cloned.1.call-start = ((), (), s32[]{:S(2)}) async-start(), calls=%async_computation.4 | async-start | bytes 147456 | tf_op jit(solution)/shard_map/reduce_scatter | solution.py:50
  295.3 6.8 collective-permute-start.2
  297.1 6.4 collective-permute-start.3
  304.2 297.4 %reduce-scatter.8.cloned.1.call-start = ((), (), s32[]{:S(2)}) async-start(), calls=%async_computation.5 | async-start | bytes 147456 | tf_op jit(solution)/shard_map/reduce_scatter | solution.py:50
  558.2 6.8 collective-permute-start.4
  560.0 6.4 collective-permute-start.5
Sparse Core Ops, SparseCore 0:
  37.5 37.8 reduce-scatter.3
  304.3 34.2 reduce-scatter.5
  567.2 34.3 reduce-scatter.7
where the time goes:
time: 717 us; the launch traced here: 715 us
  blocking collectives  562 us (78%)
  waiting for transfers between devices  110 us (15%)
  starting transfers between devices  16.1 us (2%)
  between operations  14 us (2%)
    psum x3, blocking collectives, residual_sum(): return lax.psum(local_dots(residual_now, precond_now), ('dom', 'sub'))  304 us
    psum x2, blocking collectives, local(): curvature = lax.psum(local_dots(direction, image_vec), ('dom', 'sub'))  212 us
    reduce_scatter x3, waiting for transfers between devices, local(): lax.psum_scatter(spread[:group_rows] + incoming, 'sub', scatter_dimension...  104 us
    all_gather x3, blocking collectives, local(): own_group = lax.all_gather(direction, 'sub', axis=0, tiled=True)  46.1 us
    ppermute x6, starting transfers between devices, passed_along(): return lax.ppermute(x, axis, pairs)  16 us
  transfers between devices with their start and end apart: 9, of which 8 were waited for; matrix products, arithmetic and copies ran while one was open for 1% of the time, Pallas kernels for 0%

commit v1 on v0

--- a/solution.py
+++ b/solution.py
@@ -51,7 +51,8 @@
             spread[:group_rows] + incoming, "sub", scatter_dimension=0, tiled=True
         )
         image_vec = own_part + forward + back_own
-        curvature = lax.psum(local_dots(direction, image_vec), ("dom", "sub"))
+        one_axis = lax.psum(local_dots(direction, image_vec), "dom")
+        curvature = lax.psum(one_axis, "sub")
         step_size = precond_dot / curvature
         solution_field = solution_field + step_size[None, :, None] * direction
         residual = residual - step_size[None, :, None] * image_vec

time: 717 us -> 966 us (1.35)
  blocking collectives: 562 us -> 818 us
    psum x2 -> x6, blocking collectives: 212 us -> 468 us  [the longest x3 343 us: local(): one_axis = lax.psum(local_dots(direction, image_vec), 'dom')]
where the time goes in v1:
time: 966 us; the launch traced here: 965 us
  blocking collectives  818 us (85%)
  waiting for transfers between devices  103 us (11%)
  starting transfers between devices  16.7 us (2%)
  between operations  14 us (1%)
    psum x3, blocking collectives, local(): one_axis = lax.psum(local_dots(direction, image_vec), 'dom')  343 us
    psum x3, blocking collectives, residual_sum(): return lax.psum(local_dots(residual_now, precond_now), ('dom', 'sub'))  303 us
    psum x3, blocking collectives, local(): curvature = lax.psum(one_axis, 'sub')  125 us
    reduce_scatter x3, waiting for transfers between devices, local(): lax.psum_scatter(spread[:group_rows] + incoming, 'sub', scatter_dimension...  96.8 us
    all_gather x3, blocking collectives, local(): own_group = lax.all_gather(direction, 'sub', axis=0, tiled=True)  46.1 us
  transfers between devices with their start and end apart: 9, of which 8 were waited for; matrix products, arithmetic and copies ran while one was open for 1% of the time, Pallas kernels for 0%

profile of v1, /device:TPU:1, one launch (start us, length us, event | category | flops | bytes accessed | tf_op | source)
XLA Modules:
  0.0 964.7 jit_solution(6920247303215485182)
XLA Ops:
  7.2 0.8 broadcast_divide_fusion
  8.0 19.6 %all_gather.9 = f32[16,16,128]{2,1,0:T(8,128)S(1)} all-gather(f32[2,16,128]{2,1,0:T(8,128)S(1)} %broadcast_divide_fusion), channel_id=1, replica_groups=mesh['dom'=64,'sub'=8] {'sub'}, dimensions={0}, use_global_device_ids=true | all-gather | bytes 147456 | tf_op jit(solution)/shard_map/all_gather | solution.py:42
  27.6 1.4 collective-permute-start
  30.3 4.0 collective-permute-start.1
  35.0 1.7 collective-permute-done.1
  36.7 0.7 copy_add_fusion.2
  38.2 37.2 %reduce-scatter.4.cloned.1.call-done = f32[2,16,128]{2,1,0:T(8,128)} async-done(((f32[16,16,128]{2,1,0:T(8,128)}), f32[2,16,128]{2,1,0:T(8,128)}) %reduce-scatter.4.cloned.1.call-update) | async-done | bytes 16400 | tf_op jit(solution)/shard_map/reduce_scatter | solution.py:50
  75.4 0.8 multiply_reduce_fusion.4
  76.2 105.8 %psum.63 = f32[16]{0:T(128)S(1)} all-reduce(f32[16]{0:T(128)S(1)} %get-tuple-element.3), channel_id=1, replica_groups=mesh['dom'=64,'sub'=8] {'dom','sub'}, use_global_device_ids=true, to_apply=%region_1.2 | all-reduce | flops 16 | bytes 128 | tf_op jit(solution)/shard_map/psum | solution.py:31
  182.0 112.1 %psum.64 = f32[16]{0:T(128)S(1)} all-reduce(f32[16]{0:T(128)S(1)} %get-tuple-element.2), channel_id=1, replica_groups=mesh['dom'=64,'sub'=8] {'dom'}, use_global_device_ids=true, to_apply=%region_4.5 | all-reduce | flops 16 | bytes 128 | tf_op jit(solution)/shard_map/psum | solution.py:54
  294.1 39.9 %psum.65 = f32[16]{0:T(128)S(1)} all-reduce(f32[16]{0:T(128)S(1)} %psum.64), channel_id=1, replica_groups=mesh['dom'=64,'sub'=8] {'sub'}, use_global_device_ids=true, to_apply=%region_5.6 | all-reduce | flops 16 | bytes 128 | tf_op jit(solution)/shard_map/psum | solution.py:55
  334.2 98.7 %psum.66 = f32[16]{0:T(128)S(1)} all-reduce(f32[16]{0:T(128)S(1)} %get-tuple-element.10), channel_id=1, replica_groups=mesh['dom'=64,'sub'=8] {'dom','sub'}, use_global_device_ids=true, to_apply=%region_7.8 | all-reduce | flops 16 | bytes 128 | tf_op jit(solution)/shard_map/psum | solution.py:31
  433.0 13.2 %all_gather.10 = f32[16,16,128]{2,1,0:T(8,128)S(1)} all-gather(f32[2,16,128]{2,1,0:T(8,128)S(1)} %multiply_add_fusion.2), channel_id=1, replica_groups=mesh['dom'=64,'sub'=8] {'sub'}, dimensions={0}, use_global_device_ids=true | all-gather | bytes 147456 | tf_op jit(solution)/shard_map/all_gather | solution.py:42
  446.6 1.3 collective-permute-start.2
  448.4 4.3 collective-permute-start.3
  453.0 1.1 collective-permute-done.2
  454.4 1.0 collective-permute-done.3
  456.9 29.7 %reduce-scatter.6.cloned.1.call-done = f32[2,16,128]{2,1,0:T(8,128)} async-done(((f32[16,16,128]{2,1,0:T(8,128)}), f32[2,16,128]{2,1,0:T(8,128)}) %reduce-scatter.6.cloned.1.call-update) | async-done | bytes 16400 | tf_op jit(solution)/shard_map/reduce_scatter | solution.py:50
  486.7 0.8 multiply_reduce_fusion.2
  487.5 115.7 %psum.67 = f32[16]{0:T(128)S(1)} all-reduce(f32[16]{0:T(128)S(1)} %get-tuple-element.8), channel_id=1, replica_groups=mesh['dom'=64,'sub'=8] {'dom'}, use_global_device_ids=true, to_apply=%region_10.11 | all-reduce | flops 16 | bytes 128 | tf_op jit(solution)/shard_map/psum | solution.py:54
  603.2 42.5 %psum.68 = f32[16]{0:T(128)S(1)} all-reduce(f32[16]{0:T(128)S(1)} %psum.67), channel_id=1, replica_groups=mesh['dom'=64,'sub'=8] {'sub'}, use_global_device_ids=true, to_apply=%region_11.12 | all-reduce | flops 16 | bytes 128 | tf_op jit(solution)/shard_map/psum | solution.py:55
  646.0 98.7 %psum.69 = f32[16]{0:T(128)S(1)} all-reduce(f32[16]{0:T(128)S(1)} %get-tuple-element.6), channel_id=1, replica_groups=mesh['dom'=64,'sub'=8] {'dom','sub'}, use_global_device_ids=true, to_apply=%region_13.14 | all-reduce | flops 16 | bytes 128 | tf_op jit(solution)/shard_map/psum | solution.py:31
  744.7 13.2 %all_gather.11 = f32[16,16,128]{2,1,0:T(8,128)S(1)} all-gather(f32[2,16,128]{2,1,0:T(8,128)S(1)} %multiply_add_fusion.1), channel_id=1, replica_groups=mesh['dom'=64,'sub'=8] {'sub'}, dimensions={0}, use_global_device_ids=true | all-gather | bytes 147456 | tf_op jit(solution)/shard_map/all_gather | solution.py:42
  758.3 1.3 collective-permute-start.4
  760.1 4.3 collective-permute-start.5
  764.7 1.1 collective-permute-done.4
  766.1 1.0 collective-permute-done.5
  768.6 29.9 %reduce-scatter.8.cloned.1.call-done = f32[2,16,128]{2,1,0:T(8,128)} async-done(((f32[16,16,128]{2,1,0:T(8,128)}), f32[2,16,128]{2,1,0:T(8,128)}) %reduce-scatter.8.cloned.1.call-update) | async-done | bytes 16400 | tf_op jit(solution)/shard_map/reduce_scatter | solution.py:50
  798.5 0.8 multiply_reduce_fusion
  799.3 115.6 %psum.70 = f32[16]{0:T(128)S(1)} all-reduce(f32[16]{0:T(128)S(1)} %get-tuple-element.4), channel_id=1, replica_groups=mesh['dom'=64,'sub'=8] {'dom'}, use_global_device_ids=true, to_apply=%region_16.17 | all-reduce | flops 16 | bytes 128 | tf_op jit(solution)/shard_map/psum | solution.py:54
  915.0 42.5 %psum.71 = f32[16]{0:T(128)S(1)} all-reduce(f32[16]{0:T(128)S(1)} %psum.70), channel_id=1, replica_groups=mesh['dom'=64,'sub'=8] {'sub'}, use_global_device_ids=true, to_apply=%region_17.18 | all-reduce | flops 16 | bytes 128 | tf_op jit(solution)/shard_map/psum | solution.py:55
  957.5 0.7 multiply_subtract_fusion
  (59 shorter events, 9.1 us)
Async XLA Ops:
  7.2 21.9 %copy-start = (f32[2,4,128,128]{3,2,1,0:T(8,128)S(1)}, f32[2,4,128,128]{3,2,1,0:T(8,128)}, u32[]{:S(2)}) copy-start(f32[2,4,128,128]{3,2,1,0:T(8,128)} %param.8) | copy-start | bytes 1572868
  7.2 68.2 %reduce-scatter.4.cloned.1.call-start = ((), (), s32[]{:S(2)}) async-start(), calls=%async_computation.3 | async-start | bytes 147456 | tf_op jit(solution)/shard_map/reduce_scatter | solution.py:50
  8.0 21.0 %copy-start.5 = (s32[2]{0:T(128)S(1)}, s32[2]{0:T(128)}, u32[]{:S(2)}) copy-start(s32[2]{0:T(128)} %param.10) | copy-start | bytes 28
  8.0 21.1 %copy-start.2 = (f32[2,16,128]{2,1,0:T(8,128)S(1)}, f32[2,16,128]{2,1,0:T(8,128)}, u32[]{:S(2)}) copy-start(f32[2,16,128]{2,1,0:T(8,128)} %param.6) | copy-start | bytes 49156
  27.6 1.5 copy-start.3
  27.6 7.0 collective-permute-start
  29.1 0.7 copy-start.4
  30.2 4.1 copy-start.1
  30.3 6.4 collective-permute-start.1
  37.4 449.3 %reduce-scatter.6.cloned.1.call-start = ((), (), s32[]{:S(2)}) async-start(), calls=%async_computation.4 | async-start | bytes 147456 | tf_op jit(solution)/shard_map/reduce_scatter | solution.py:50
  446.6 7.5 collective-permute-start.2
  448.4 7.0 collective-permute-start.3
  456.1 342.4 %reduce-scatter.8.cloned.1.call-start = ((), (), s32[]{:S(2)}) async-start(), calls=%async_computation.5 | async-start | bytes 147456 | tf_op jit(solution)/shard_map/reduce_scatter | solution.py:50
  758.3 7.5 collective-permute-start.4
  760.1 7.0 collective-permute-start.5
Sparse Core Ops, SparseCore 0:
  37.5 37.8 reduce-scatter.3
  456.3 30.3 reduce-scatter.5
  768.0 30.4 reduce-scatter.7
